TPU v7x, 32 devices: a whole 2x2x4 slice. The times are simulated.
32 devices in a mesh: dp: 8 (over z, x), mp: 4 (over y, core).
Axes of the slice: x: 2, y: 2, z: 4, core: 2. Of those that a mesh axis runs over, the one named last changes fastest.
Arguments:
- images: bfloat16 [2, 8, 608, 1024], P(None, 'dp', 'mp'), may hold values from -6 to 6
- counts: int32 [2, 8], P(None, 'dp'), may hold values from 0 to 1, as said below
- first_gain: bfloat16 [1024], P('dp'), may hold values from 0.5 to 1.5
- first_shift: bfloat16 [1024], P('dp'), may hold values from -1.796875 to 1.796875
- query_weight: bfloat16 [1024, 1024], P('dp', 'mp'), may hold values from -0.375 to 0.375
- query_bias: bfloat16 [4, 256], P('mp', 'dp'), may hold values from -3 to 3
- key_weight: bfloat16 [1024, 1024], P('dp', 'mp'), may hold values from -0.1875 to 0.1875
- value_weight: bfloat16 [1024, 1024], P('dp', 'mp'), may hold values from -0.1875 to 0.1875
- value_bias: bfloat16 [4, 256], P('mp', 'dp'), may hold values from -3 to 3
- out_weight: bfloat16 [1024, 1024], P('dp', 'mp'), may hold values from -1 to 1
- out_bias: bfloat16 [1024], P('dp'), may hold values from -1.796875 to 1.796875
- second_gain: bfloat16 [1024], P('dp'), may hold values from 0.5 to 1.5
- second_shift: bfloat16 [1024], P('dp'), may hold values from -1.796875 to 1.796875
- up_weight: bfloat16 [1024, 4096], P('dp', 'mp'), may hold values from -0.1875 to 0.1875
- up_bias: bfloat16 [4, 1024], P('mp', 'dp'), may hold values from -3 to 3
- down_weight: bfloat16 [1024, 4096], P('dp', 'mp'), may hold values from -0.09375 to 0.09375
- down_bias: bfloat16 [1024], P('dp'), may hold values from -1.796875 to 1.796875
- clip_tau: float32 [], replicated, may hold values from 3.5 to 5.5
- out_grad: bfloat16 [2, 8, 608, 1024], P(None, 'dp', 'mp'), may hold values from -6 to 6
Outputs:
- result: bfloat16 [2, 8, 608, 1024], P(None, 'dp', 'mp')
- input_grad: bfloat16 [2, 8, 608, 1024], P(None, 'dp', 'mp')
- first_gain_grad: float32 [1024], P('dp')
- first_shift_grad: float32 [1024], P('dp')
- query_weight_grad: float32 [1024, 1024], P('dp', 'mp')
- query_bias_grad: float32 [4, 256], P('mp', 'dp')
- key_weight_grad: float32 [1024, 1024], P('dp', 'mp')
- value_weight_grad: float32 [1024, 1024], P('dp', 'mp')
- value_bias_grad: float32 [4, 256], P('mp', 'dp')
- out_weight_grad: float32 [1024, 1024], P('dp', 'mp')
- out_bias_grad: float32 [1024], P('dp')
- second_gain_grad: float32 [1024], P('dp')
- second_shift_grad: float32 [1024], P('dp')
- up_weight_grad: float32 [1024, 4096], P('dp', 'mp')
- up_bias_grad: float32 [4, 1024], P('mp', 'dp')
- down_weight_grad: float32 [1024, 4096], P('dp', 'mp')
- down_bias_grad: float32 [1024], P('dp')
- logit_peaks: float32 [16], P('mp')
- clipped_query: float32 [1024, 1024], P('dp', 'mp')
- clipped_key: float32 [1024, 1024], P('dp', 'mp')
- clipped_bias: float32 [4, 256], P('mp', 'dp')
Inputs may be any that keep to these rules, and one draw needn't show every extreme that they name: The first counts[b, j] slots of index j hold images; in every micro-batch some index holds an image and some holds none.
All inputs are finite; a program needn't handle non-finite values.
Results may differ from a plain program's by a relative error of at most 0.012.
The roundings to bfloat16 on the way count: a program that leaves them out, or rounds other values in their place, can miss the bound.
Values may be sent and summed in bfloat16 or wider, within the bound.
A program may use at most 192 MiB of HBM per device.

v0:
```python
import functools
import math

import jax
import jax.numpy as jnp
from jax import lax
from jax.experimental import pallas as pl
from jax.experimental.pallas import tpu as pltpu
from jax.sharding import PartitionSpec as P

HD = 64
IMG_LEN = 577
F32 = jnp.float32
BF16 = jnp.bfloat16
MESH = pl.DeviceIdType.MESH
TILE = 256
PQ, PK, PV, PO = 0, 1, 2, 3
PAIR_FIRST = (6, 9)
LINE_FIRST = (4, 5)
DIRECT = (0, 1)
G1, S1, OB, G2, S2, DB, UB, QB, VB = 0, 1, 2, 3, 4, 5, 6, 8, 9
DG1, DS1, DOB, DG2, DS2, DDB, DUB, DQB, DVB, PEAK = 0, 1, 2, 3, 4, 5, 6, 7, 8, 9


def dot_nn(left, right):
    return lax.dot_general(left, right, (((1,), (0,)), ((), ())), preferred_element_type=F32)


def dot_nt(left, right):
    return lax.dot_general(left, right, (((1,), (1,)), ((), ())), preferred_element_type=F32)


def dot_tn(left, right):
    return lax.dot_general(left, right, (((0,), (0,)), ((), ())), preferred_element_type=F32)


def standardize(rows):
    center = rows - jnp.mean(rows, axis=-1, keepdims=True)
    inverse = lax.rsqrt(jnp.mean(center * center, axis=-1, keepdims=True) + 1e-05)
    return center * inverse, inverse


def norm_back(incoming, scaled, inverse, gain):
    upward = incoming * gain
    return inverse * (
        upward
        - jnp.mean(upward, axis=-1, keepdims=True)
        - scaled * jnp.mean(upward * scaled, axis=-1, keepdims=True)
    )


def each(low, high, body):
    if high - low <= 8:
        for at in range(low, high):
            body(at)
    else:

        def step(at, carry):
            body(at)
            return carry

        lax.fori_loop(low, high, step, 0)


def tiles(width, body, at_once=2):
    def step(at, carry):
        for more in range(at_once):
            body(at_once * at + more)
        return carry

    lax.fori_loop(0, width // (at_once * TILE), step, 0)


def sum_rows(rows):
    return jnp.sum(rows, axis=0, keepdims=True)


class Layer:
    def __init__(self, size, refs):
        self.__dict__.update(size)
        self.__dict__.update(refs)
        self.dp_at = lax.axis_index("dp")
        self.mp_at = lax.axis_index("mp")
        self.line_at = self.dp_at // 2
        self.pair_at = lax.rem(self.dp_at, 2)
        self.chip_at = self.mp_at // 2
        self.core_at = lax.rem(self.mp_at, 2)
        self.sib = (self.dp_at, self.chip_at * 2 + 1 - self.core_at)
        self.across = (self.dp_at, (1 - self.chip_at) * 2 + self.core_at)
        self.pair = (self.line_at * 2 + 1 - self.pair_at, self.mp_at)
        self.middle = (self.line_at == 1) | (self.line_at == 2)
        self.pieces = 4 + 2 * self.chunks
        self.pair_first = PAIR_FIRST if self.lines == 4 else ()
        self.line_first = LINE_FIRST if self.lines == 4 else ()
        self.pair_slots = (self.pieces - len(self.line_first)) * self.lines
        self.rest = None
        self.stage_sends = [[], []]
        self.spread_sends = [[], [], [], []]
        self.late = []

    def line_of(self, step):
        return lax.rem(self.line_at + step + self.lines, self.lines)

    def line_peer(self, step):
        return (self.line_of(step) * 2 + self.pair_at, self.mp_at)

    def slot(self, line, pair):
        return pl.ds(pl.multiple_of((line * 2 + pair) * self.shard, self.shard), self.shard)

    def block(self, micro, chip, core):
        start = micro * self.rows + (chip * 2 + core) * self.pad
        return pl.ds(pl.multiple_of(start, 16), self.pad)

    def own_block(self, micro):
        return self.block(micro, self.chip_at, self.core_at)

    def source(self, piece):
        if piece < 4:
            return (self.query_w, self.key_w, self.value_w, self.out_w)[piece]
        which, chunk = (piece - 4) % 2, (piece - 4) // 2
        return (self.up_w, self.down_w)[which].at[:, pl.ds(chunk * TILE, TILE)]

    def copy(self, src, dst, send_sem, recv_sem, device):
        return pltpu.make_async_remote_copy(
            src_ref=src,
            dst_ref=dst,
            send_sem=send_sem,
            recv_sem=recv_sem,
            device_id=device,
            device_id_type=MESH,
        )

    def channels(self, piece):
        if piece in self.pair_first:
            return ((piece, False), (self.pieces + self.pair_first.index(piece), True))
        return ((piece, False),)

    def shard_place(self, piece, line, other):
        pair = 1 - self.pair_at if other else self.pair_at
        return self.weights.at[piece, self.slot(line, pair)]

    def broad(self, piece, channel, other, step):
        place = self.shard_place(piece, self.line_at, other)
        return self.copy(
            place if other else self.source(piece),
            place,
            self.wz_send.at[channel, step - 1],
            self.wz_recv.at[channel, step - 1],
            self.line_peer(step),
        )

    def broad_in(self, piece, channel, other, step):
        place = self.shard_place(piece, self.line_of(-step), other)
        return self.copy(
            place,
            place,
            self.wz_send.at[channel, step - 1],
            self.wz_recv.at[channel, step - 1],
            self.line_peer(-step),
        )

    def broad_each(self, piece, channel, other, act):
        def one(step):
            if self.lines == 4 and step != 2:
                @pl.when(self.line_at != (3 if step == 1 else 0))
                def _():
                    act(self.broad(piece, channel, other, step))
            else:
                act(self.broad(piece, channel, other, step))

        each(1, self.lines, one)

    def relay(self, piece, channel, other, act):
        if self.lines != 4:
            return

        @pl.when(self.middle)
        def _():
            place = self.shard_place(piece, 3 * (2 - self.line_at), other)
            end = (3 * (self.line_at - 1) * 2 + self.pair_at, self.mp_at)
            act(
                self.copy(
                    place,
                    place,
                    self.wz_send.at[channel, 3],
                    self.wz_recv.at[channel, 2 * (self.line_at - 1)],
                    end,
                )
            )

    def weight_pair(self, piece, step, own):
        place = self.shard_place(piece, self.line_of(-step), False)
        return self.copy(
            self.source(piece) if own else place,
            place,
            self.wx_send.at[piece, step],
            self.wx_recv.at[piece, step],
            self.pair,
        )

    def weight_pair_in(self, piece, step):
        place = self.shard_place(piece, self.line_of(-step), True)
        return self.copy(
            place, place, self.wx_send.at[piece, step], self.wx_recv.at[piece, step], self.pair
        )

    def weight_local(self, piece):
        return pltpu.make_async_copy(
            self.source(piece),
            self.shard_place(piece, self.line_at, False),
            self.wl_sem.at[piece],
        )

    def send_pair(self, piece):
        self.weight_pair(piece, 0, True).start()

    def send_weight(self, piece, pair=True):
        if pair:
            self.send_pair(piece)
        self.broad_each(piece, piece, False, lambda one: one.start())
        self.weight_local(piece).start()

    def pass_weight(self, piece):
        self.flush()
        if piece in self.pair_first:
            self.weight_pair_in(piece, 0).wait_recv()
            channel, other = self.channels(piece)[1]
            self.broad_each(piece, channel, other, lambda one: one.start())
            return

        def one(step, last=False):
            self.broad_in(piece, piece, False, step).wait_recv()
            if last:
                self.relay(piece, piece, False, lambda one: one.start())
            self.weight_pair(piece, step, False).start()

        if self.lines == 4:
            second = jnp.where(self.line_at < 2, 3, 1)
            one(2, True)
            one(second)
            self.rest = lambda: one(4 - second)
        else:
            each(1, self.lines, one)

    def flush(self):
        if self.rest is not None:
            self.rest()
        self.rest = None

    def relay_weight(self, piece):
        for channel, other in self.channels(piece):
            if piece in self.pair_first:
                self.broad_in(piece, channel, other, 2).wait_recv()
                self.relay(piece, channel, other, lambda one: one.start())

    def await_weight(self, piece):
        self.weight_local(piece).wait()
        if piece in self.pair_first:
            for channel, other in self.channels(piece):
                for step in (1, 3):
                    self.broad_in(piece, channel, other, step).wait_recv()
        else:
            each(0, self.lines, lambda step: self.weight_pair_in(piece, step).wait_recv())

    def weight_sent(self, piece):
        self.weight_pair(piece, 0, True).wait_send()
        for channel, other in self.channels(piece):
            self.broad_each(piece, channel, other, lambda one: one.wait_send())
            self.relay(piece, channel, other, lambda one: one.wait_send())
        if piece not in self.pair_first:
            each(1, self.lines, lambda step: self.weight_pair(piece, step, False).wait_send())

    def spread_copy(self, kind, micro, ref, which):
        place = ref.at[self.own_block(micro)]
        if which == 2:
            place = ref.at[self.block(micro, 1 - self.chip_at, self.core_at)]
        return self.copy(
            place,
            place,
            self.ag_send.at[kind, micro, which],
            self.ag_recv.at[kind, micro, which],
            self.across if which == 0 else self.sib,
        )

    def spread_in(self, kind, micro, ref, which):
        chip = self.chip_at if which == 1 else 1 - self.chip_at
        core = self.core_at if which == 0 else 1 - self.core_at
        place = ref.at[self.block(micro, chip, core)]
        return self.copy(
            place,
            place,
            self.ag_send.at[kind, micro, which],
            self.ag_recv.at[kind, micro, which],
            self.across if which == 0 else self.sib,
        )

    def spread(self, kind, micro, ref):
        for which in (0, 1):
            self.spread_copy(kind, micro, ref, which).start()
            self.spread_sends[kind].append((micro, ref, which))

    def spread_on(self, kind, micro, ref):
        self.spread_in(kind, micro, ref, 0).wait_recv()
        self.spread_copy(kind, micro, ref, 2).start()
        self.spread_sends[kind].append((micro, ref, 2))

    def spread_sent(self, kind):
        for micro, ref, which in self.spread_sends[kind]:
            self.spread_copy(kind, micro, ref, which).wait_send()
        self.spread_sends[kind] = []

    def spread_end(self, kind, micro, ref):
        self.spread_in(kind, micro, ref, 1).wait_recv()
        self.spread_in(kind, micro, ref, 2).wait_recv()

    def collect(self, kind, micro, terms):
        for one in self.stage_sends[micro]:
            one.wait_send()
        self.stage_sends[micro] = []
        held = 1 if kind == 1 else 0
        for half, chip in ((0, 1 - self.chip_at), (1, self.chip_at)):
            start = pl.multiple_of(micro * self.rows + chip * 2 * self.pad, 16)
            stage, keep = self.stage.at[micro, half], self.keep.at[held, micro, half]

            def tile_of(tile):
                cols = pl.ds(pl.multiple_of(tile * TILE, TILE), TILE)
                product = terms(pl.ds(start, 2 * self.pad), cols)
                low, high = product[: self.pad], product[self.pad :]
                keep[:, cols] = jnp.where(self.core_at == 0, low, high)
                stage[:, cols] = jnp.where(self.core_at == 0, high, low).astype(BF16)

            tiles(self.width, tile_of, 1 if kind == 1 else 4)
            one = self.copy(
                stage,
                self.sib_in.at[kind, micro, half],
                self.rs_send.at[kind, micro, half],
                self.rs_recv.at[kind, micro, half],
                self.sib,
            )
            one.start()
            self.stage_sends[micro].append(one)

    def collect_far(self, kind, micro):
        incoming = self.sib_in.at[kind, micro, 0]
        self.copy(
            incoming,
            incoming,
            self.rs_send.at[kind, micro, 0],
            self.rs_recv.at[kind, micro, 0],
            self.sib,
        ).wait_recv()
        held = self.keep[1 if kind == 1 else 0, micro, 0]
        incoming[...] = (held + incoming[...].astype(F32)).astype(BF16)
        one = self.copy(
            incoming,
            self.far_in.at[kind, micro],
            self.rs_send.at[kind, micro, 2],
            self.rs_recv.at[kind, micro, 2],
            self.across,
        )
        one.start()
        self.late.append(one)

    def collected(self, kind, micro):
        near, far = self.sib_in.at[kind, micro, 1], self.far_in.at[kind, micro]
        self.copy(
            near, near, self.rs_send.at[kind, micro, 1], self.rs_recv.at[kind, micro, 1], self.sib
        ).wait_recv()
        self.copy(
            far, far, self.rs_send.at[kind, micro, 2], self.rs_recv.at[kind, micro, 2], self.across
        ).wait_recv()
        total = self.keep[1 if kind == 1 else 0, micro, 1] + near[...].astype(F32)
        return (total + far[...].astype(F32))[: self.part]

    def summed(self, piece):
        if piece < 4:
            return self.proj_back.at[: self.width, piece * TILE : (piece + 1) * TILE]
        return self.wide_sums.at[piece - 4]

    def sum_place(self, piece, line, other):
        pair = 1 - self.pair_at if other else self.pair_at
        return self.summed(piece).at[self.slot(line, pair)]

    def sum_channels(self, piece):
        if piece in self.line_first:
            return ((piece, False), (self.pieces + self.line_first.index(piece), True))
        return ((piece, False),)

    def relayed(self, piece):
        return self.lines == 4 and piece not in DIRECT

    def out_columns(self, piece):
        at = piece if piece < 4 else 4 + self.chunks * ((piece - 4) % 2) + (piece - 4) // 2
        return self.weight_g.at[:, pl.ds(at * TILE, TILE)]

    def pair_place(self, piece, line):
        if piece in self.line_first:
            return self.pair_in.at[self.pair_slots + self.line_first.index(piece)]
        before = sum(1 for other in self.line_first if other < piece)
        return self.pair_in.at[(piece - before) * self.lines + line]

    def grad_pair(self, piece, line):
        at = 0 if piece in self.line_first else line
        return self.copy(
            self.sum_place(piece, line, True),
            self.pair_place(piece, line),
            self.gx_send.at[piece, at],
            self.gx_recv.at[piece, at],
            self.pair,
        )

    def line_source(self, piece, line, other):
        if piece in self.line_first:
            return self.sum_place(piece, line, other)
        return self.pair_place(piece, line)

    def grad_line(self, piece, channel, other, step):
        line = self.line_of(step)
        target, at = line, step - 1
        if self.relayed(piece) and step != 2:
            far = self.line_at == (3 if step == 1 else 0)
            target = jnp.where(far, 2 if step == 1 else 1, line)
            at = jnp.where(far, 3, step - 1)
        return self.copy(
            self.line_source(piece, line, other),
            self.line_in.at[channel, at],
            self.gz_send.at[channel, step - 1],
            self.gz_recv.at[channel, at],
            (target * 2 + self.pair_at, self.mp_at),
        )

    def grad_line_in(self, channel, at):
        place = self.line_in.at[channel, at]
        return self.copy(
            place, place, self.gz_send.at[channel, 0], self.gz_recv.at[channel, at], self.pair
        )

    def grad_make(self, piece, left, right, send=True):
        out = self.summed(piece)

        def one(tile):
            cols = pl.ds(pl.multiple_of(tile * TILE, TILE), TILE)
            out[cols, :] = dot_tn(left[:, cols], right).astype(BF16)

        tiles(self.width, one)
        if send:
            self.grad_send(piece)

    def grad_send(self, piece):
        if piece in self.line_first:
            for channel, other in self.sum_channels(piece):
                for step in (1, 3):
                    self.grad_line(piece, channel, other, step).start()

                @pl.when(jnp.logical_not(self.middle))
                def _():
                    self.grad_line(piece, channel, other, 2).start()
        else:
            each(0, self.lines, lambda line: self.grad_pair(piece, line).start())

    def grad_pass(self, piece):
        def one(step, wait=True):
            line = self.line_of(step)
            if wait:
                self.grad_pair(piece, line).wait_recv()
            ref = self.pair_place(piece, line)
            total = self.sum_place(piece, line, False)[...].astype(F32) + ref[...].astype(F32)
            ref[...] = total.astype(BF16)
            self.grad_line(piece, piece, False, step).start()

        if piece in self.line_first:
            return
        if self.relayed(piece):
            one(1)
            one(3)
            self.grad_pair(piece, self.line_of(2)).wait_recv()
            pl.when(jnp.logical_not(self.middle))(lambda: one(2, False))
        else:
            each(1, self.lines, one)

    def grad_relay(self, piece):
        if not self.relayed(piece):
            return

        @pl.when(self.middle)
        def _():
            for channel, other in self.sum_channels(piece):
                line = self.line_of(2)
                self.grad_line_in(channel, 3).wait_recv()
                ref = self.line_source(piece, line, other)
                total = ref[...].astype(F32) + self.line_in[channel, 3].astype(F32)
                if piece not in self.line_first:
                    total = total + self.sum_place(piece, line, False)[...].astype(F32)
                ref[...] = total.astype(BF16)
                self.grad_line(piece, channel, other, 2).start()

    def line_total(self, piece, channel, ref):
        for step in range(1, self.lines):

            def one():
                self.grad_line_in(channel, step - 1).wait_recv()
                ref[...] += self.line_in[channel, step - 1].astype(F32)

            if self.relayed(piece) and step != 2:
                pl.when(self.line_at != (0 if step == 1 else 3))(one)
            else:
                one()

    def grad_cross(self, piece):
        if piece not in self.line_first:
            return
        ref = self.sum_place(piece, self.line_at, True)
        total = self.out_columns(piece)
        total[...] = ref[...].astype(F32)
        self.line_total(piece, self.sum_channels(piece)[1][0], total)
        ref[...] = total[...].astype(BF16)
        self.grad_pair(piece, self.line_at).start()

    def grad_end(self, piece):
        ref = self.out_columns(piece)
        self.grad_pair(piece, self.line_at).wait_recv()
        came = self.pair_place(piece, self.line_at)[...].astype(F32)
        ref[...] = self.sum_place(piece, self.line_at, False)[...].astype(F32) + came
        self.line_total(piece, piece, ref)

    def grad_sent(self, piece):
        if piece in self.line_first:
            self.grad_pair(piece, self.line_at).wait_send()
        else:
            each(0, self.lines, lambda line: self.grad_pair(piece, line).wait_send())
        for channel, other in self.sum_channels(piece):
            each(
                1,
                self.lines,
                lambda step: self.grad_line(piece, channel, other, step).wait_send(),
            )

    def clip(self, peaks):
        root = jnp.sqrt(self.tau[0, 0] / jnp.maximum(peaks, self.tau[0, 0]))
        head = lax.broadcasted_iota(jnp.int32, (1, TILE), 1) // HD
        roots = jnp.zeros((1, TILE), F32)
        for at in range(self.heads):
            roots = jnp.where(head == at, root[:, at : at + 1], roots)
        first = (4 + 2 * self.chunks) * TILE
        mine = self.slot(self.line_at, self.pair_at)
        for at, piece in enumerate((PQ, PK)):
            cols = slice(first + at * TILE, first + (at + 1) * TILE)
            self.weight_g[:, cols] = self.weights[piece, mine, :].astype(F32) * roots
        low, high = self.own_packed[8:9, :], self.own_packed[9:10, :]
        bias = low * roots[:, 0:128] + high * roots[:, 128:256]
        return bias

    def vector_copy(self, step):
        return self.copy(
            self.own_packed,
            self.vectors_in.at[self.dp_at],
            self.v_send.at[0, step - 1],
            self.v_recv.at[0, step - 1],
            (lax.rem(self.dp_at + step, self.dps), self.mp_at),
        )

    def vector_copy_in(self, step):
        origin = lax.rem(self.dp_at - step + self.dps, self.dps)
        place = self.vectors_in.at[origin]
        return self.copy(
            place,
            place,
            self.v_send.at[0, step - 1],
            self.v_recv.at[0, step - 1],
            (origin, self.mp_at),
        )

    def share_copy(self, step):
        target = lax.rem(self.dp_at + step, self.dps)
        return self.copy(
            self.shares.at[target],
            self.shares_in.at[step - 1],
            self.v_send.at[1, step - 1],
            self.v_recv.at[1, step - 1],
            (target, self.mp_at),
        )

    def group_copy(self, step):
        return self.copy(
            self.group.at[0],
            self.group.at[step],
            self.m_send.at[step - 1],
            self.m_recv.at[step - 1],
            (self.dp_at, lax.rem(self.mp_at + step, 4)),
        )

    def pack_vectors(self):
        if not self.own_vectors:
            return
        rows = [ref[...].astype(F32) for ref in self.small[:7]] + [jnp.zeros((1, 128), F32)]
        shift = lax.rem(self.dp_at * 32, 128)
        for ref in self.small[7:]:
            wide = jnp.concatenate([ref[...].astype(F32), jnp.zeros((1, 96), F32)], axis=1)
            wide = pltpu.roll(wide, shift, 1)
            rows.append(jnp.where(self.dp_at < 4, wide, 0.0))
            rows.append(jnp.where(self.dp_at < 4, 0.0, wide))
        self.own_packed[...] = jnp.concatenate(rows + [jnp.zeros((4, 128), F32)], axis=0)

    def take_vectors(self):
        if not self.own_vectors:
            self.vectors[...] = self.small[0][...]
            return
        self.vectors_in[self.dp_at] = self.own_packed[...]
        for step in range(1, self.dps):
            self.vector_copy_in(step).wait_recv()
        rest = self.vectors_in[0, 8:16, :]
        for at in range(1, self.dps):
            rest = rest + self.vectors_in[at, 8:16, :]
        for at in range(self.dps):
            self.vectors[0:8, at * 128 : (at + 1) * 128] = self.vectors_in[at, 0:8, :]
        for row, first in ((QB, 0), (VB, 2)):
            self.vectors[row : row + 1, 0:128] = rest[first : first + 1]
            self.vectors[row : row + 1, 128:256] = rest[first + 1 : first + 2]

    def give_vectors(self):
        if not self.own_vectors:
            self.vector_g[...] = self.sums[...]
            return
        for at in range(self.dps):
            half = (at * 32 // 128) * 128
            self.shares[at, 0:7, :] = self.sums[0:7, at * 128 : (at + 1) * 128]
            self.shares[at, 7:9, :] = self.sums[7:9, half : half + 128]
            self.shares[at, 9:16, :] = self.sums[9:16, 0:128]
        for step in range(1, self.dps):
            self.share_copy(step).start()

    def end_vectors(self):
        if not self.own_vectors:
            return
        total = self.shares[self.dp_at]
        most = total[PEAK : PEAK + 1]
        for step in range(1, self.dps):
            self.share_copy(step).wait_recv()
            came = self.shares_in[step - 1]
            total = total + came
            most = jnp.maximum(most, came[PEAK : PEAK + 1])
        self.group[0] = jnp.concatenate([total[:PEAK], most, total[PEAK + 1 :]], axis=0)
        for step in range(1, 4):
            self.group_copy(step).start()

    def last_vectors(self):
        if not self.own_vectors:
            return
        total = self.group[0]
        most = total[PEAK : PEAK + 1]
        whole = total[0:6]
        for step in range(1, 4):
            self.group_copy(step).wait_recv()
            whole = whole + self.group[step, 0:6, :]
        narrow = jnp.concatenate([total[7:9], self.clip(most), jnp.zeros((5, 128), F32)], axis=0)
        shift = lax.rem(128 - lax.rem(self.dp_at * 32, 128), 128)
        narrow = pltpu.roll(narrow, shift, 1)
        self.vector_g[0:6, :] = whole
        self.vector_g[6:7, :] = total[6:7]
        self.vector_g[7:9, :] = narrow[0:2]
        self.vector_g[9:10, :] = most
        self.vector_g[10:11, :] = narrow[2:3]
        self.vector_g[11:16, :] = jnp.zeros((5, 128), F32)

    def vector(self, row, start=0, size=None):
        size = self.width if size is None else size
        return self.vectors[row : row + 1, pl.ds(start, size)]

    def add_sum(self, row, value, start=0):
        cols = pl.ds(start, value.shape[1])
        self.sums[row : row + 1, cols] = self.sums[row : row + 1, cols] + value

    def mask(self, micro):
        row = self.mp_at * self.part + lax.broadcasted_iota(jnp.int32, (self.part, 1), 0)
        live = jnp.where(self.counts[micro] > 0, 1.0, 0.0).astype(F32)
        return jnp.where(row < IMG_LEN, live, 0.0)

    def put_rows(self, ref, micro, rows):
        filler = jnp.zeros((self.pad - self.part, self.width), F32)
        ref[self.own_block(micro), :] = jnp.concatenate([rows, filler], axis=0).astype(BF16)

    def first_norm(self, micro):
        scaled, _ = standardize(self.images[micro, 0].astype(F32))
        self.put_rows(self.normed_one, micro, scaled * self.vector(G1) + self.vector(S1))
        self.spread(0, micro, self.normed_one)

    def out_rows(self, micro):
        return self.out_grad[micro, 0].astype(F32) * self.mask(micro)

    def project_back(self, micro):
        rows = self.out_rows(micro)
        self.put_rows(self.proj_back, micro, rows)
        self.add_sum(DDB, sum_rows(rows.astype(BF16).astype(F32)))
        self.spread(2, micro, self.proj_back)

    def second_norm(self, micro):
        rows = self.images[micro, 0].astype(F32) + self.collected(0, micro) + self.vector(OB)
        self.after_attn[micro] = rows
        scaled, _ = standardize(rows)
        self.put_rows(self.normed_two, micro, scaled * self.vector(G2) + self.vector(S2))
        self.spread(1, micro, self.normed_two)

    def give_result(self, micro):
        rows = self.after_attn[micro] + self.collected(1, micro) + self.vector(DB)
        self.rows_g[0, micro, 0] = (self.mask(micro) * rows).astype(BF16)

    def second_norm_back(self, micro):
        incoming = self.collected(2, micro)
        scaled, inverse = standardize(self.after_attn[micro])
        rows = self.out_rows(micro) + norm_back(incoming, scaled, inverse, self.vector(G2))
        self.attn_back[micro] = rows
        self.add_sum(DOB, sum_rows(rows.astype(BF16).astype(F32)))
        self.add_sum(DG2, sum_rows(incoming * scaled))
        self.add_sum(DS2, sum_rows(incoming))
        self.put_rows(self.attended_back, micro, rows)
        self.spread(3, micro, self.attended_back)

    def first_norm_back(self, micro):
        incoming = self.collected(3, micro)
        scaled, inverse = standardize(self.images[micro, 0].astype(F32))
        self.add_sum(DG1, sum_rows(incoming * scaled))
        self.add_sum(DS1, sum_rows(incoming))
        rows = self.attn_back[micro] + norm_back(incoming, scaled, inverse, self.vector(G1))
        self.rows_g[1, micro, 0] = rows.astype(BF16)

    def image_rows(self, micro):
        return pl.ds(micro * self.rows, self.rows)

    def counted(self, axis):
        shape = (self.rows, 1) if axis == 0 else (1, self.rows)
        row = lax.broadcasted_iota(jnp.int32, shape, axis)
        block = row // self.pad
        inside = row - block * self.pad
        return (inside < self.part) & (block * self.part + inside < IMG_LEN)

    def head_columns(self, head):
        column = lax.broadcasted_iota(jnp.int32, (self.rows, TILE), 1)
        return column // HD == head

    def project_heads(self, micro):
        scale = 1.0 / math.sqrt(HD)
        part = self.rows // 2

        def half(at, carry):
            rows = pl.ds(pl.multiple_of(micro * self.rows + at * part, 16), part)
            normed = self.normed_one[rows, :]
            query = dot_nn(normed, self.weights[PQ]) + self.vector(QB, 0, TILE)
            self.queries[rows, :] = (query.astype(BF16).astype(F32) * scale).astype(BF16)
            self.keys[rows, :] = dot_nn(normed, self.weights[PK]).astype(BF16)
            value = dot_nn(normed, self.weights[PV]) + self.vector(VB, 0, TILE)
            self.values[rows, :] = value.astype(BF16)
            return carry

        lax.fori_loop(0, 2, half, 0)

    def attend(self, micro, between):
        rows = self.image_rows(micro)
        values = self.turned.at[:, : self.rows]
        values[...] = self.values[rows, :].T
        live = jnp.where(self.counts[micro] > 0, 0.0, -1e30).astype(F32)
        split = (self.rows // 2 + 127) // 128 * 128

        def one_head(head):
            query = jnp.where(self.head_columns(head), self.queries[rows, :], jnp.zeros((), BF16))
            cols = pl.ds(pl.multiple_of(head * HD, HD), HD)
            top = total = mixed = None
            for low, high in ((0, split), (split, self.rows)):
                part = pl.ds(micro * self.rows + low, high - low)
                scores = dot_nt(self.keys[part, :], query)
                scores = jnp.where(self.counted(0)[low:high], scores, -1e30)
                most = jnp.max(scores, axis=0, keepdims=True)
                if top is None:
                    expo = jnp.exp(scores - most)
                    total = jnp.sum(expo, axis=0, keepdims=True)
                    mixed = dot_nn(values[cols, low:high], expo.astype(BF16))
                    top = most
                else:
                    most = jnp.maximum(top, most)
                    again = jnp.exp(top - most)
                    expo = jnp.exp(scores - most)
                    total = total * again + jnp.sum(expo, axis=0, keepdims=True)
                    added = dot_nn(values[cols, low:high], expo.astype(BF16))
                    mixed = mixed * again + added
                    top = most
            self.log_total[micro, pl.ds(head, 1), :] = top + jnp.log(total)
            self.mixed_turned[micro, cols, :] = mixed * (1.0 / total)
            peak = jnp.max(jnp.where(self.counted(1), top, -1e30), axis=1, keepdims=True)
            peak = jnp.where(live < 0.0, -1e30, peak)
            lane = lax.broadcasted_iota(jnp.int32, (1, 128), 1)
            seen = self.sums[PEAK : PEAK + 1, 0:128]
            self.sums[PEAK : PEAK + 1, 0:128] = jnp.where(
                lane == head, jnp.maximum(seen, peak), seen
            )

        def two_heads(at, carry):
            pl.when(at == 1)(between)
            one_head(2 * at)
            one_head(2 * at + 1)
            return carry

        lax.fori_loop(0, self.heads // 2, two_heads, 0)
        self.mixed[rows, :] = self.mixed_turned[micro].T.astype(BF16)

    def attend_back(self, micro, between):
        rows = self.image_rows(micro)
        self.mixed_back[...] = dot_nn(self.attended_back[rows, :], self.weights[PO]).astype(BF16)
        keys = self.turned.at[:, : self.rows]
        outwards = self.turned.at[:, self.rows :]
        keys[...] = self.keys[rows, :].T
        outwards[...] = self.mixed_back[...].T
        self.key_sum[...] = jnp.zeros_like(self.key_sum)
        self.value_sum[...] = jnp.zeros_like(self.value_sum)
        chunk = self.rows // 2

        def one_head(head, carry):
            columns = self.head_columns(head)
            none = jnp.zeros((), BF16)
            query = jnp.where(columns, self.queries[rows, :], none)
            outward = jnp.where(columns, self.mixed_back[...], none)
            cols = pl.ds(pl.multiple_of(head * HD, HD), HD)
            dots = outwards[cols, :].astype(F32) * self.mixed_turned[micro, cols, :]
            delta = jnp.sum(dots, axis=0, keepdims=True)
            log_total = self.log_total[micro, pl.ds(head, 1), :]
            for at in range(2):
                part = pl.ds(micro * self.rows + at * chunk, chunk)
                here = pl.ds(at * chunk, chunk)
                scores = dot_nt(self.keys[part, :], query)
                counted = self.counted(0)[at * chunk : (at + 1) * chunk]
                probs = jnp.where(counted, jnp.exp(scores - log_total), 0.0)
                prob_back = dot_nt(self.values[part, :], outward)
                self.probs[here, :] = probs.astype(BF16)
                self.score_back[here, :] = (probs * (prob_back - delta)).astype(BF16)
            self.value_sum[...] += dot_nn(self.probs[...], outward)
            self.key_sum[...] += dot_nn(self.score_back[...], query)
            self.mixed_turned[micro, cols, :] = dot_nn(keys[cols, :], self.score_back[...])
            return carry

        def with_between(head, carry):
            pl.when(head == self.heads // 2)(between)
            return one_head(head, carry)

        if micro == 0:
            lax.fori_loop(0, self.heads // 2, one_head, 0)
            between()
            lax.fori_loop(self.heads // 2, self.heads, one_head, 0)
        else:
            lax.fori_loop(0, self.heads, with_between, 0)
        scale = 1.0 / math.sqrt(HD)
        query_back = (self.mixed_turned[micro] * scale).T.astype(BF16)
        value_back = self.value_sum[...].astype(BF16)
        self.queries[rows, :] = query_back
        self.keys[rows, :] = self.key_sum[...].astype(BF16)
        self.values[rows, :] = value_back
        self.add_sum(DQB, sum_rows(query_back.astype(F32)))
        self.add_sum(DVB, sum_rows(value_back.astype(F32)))

    def feed(self, micro, chunk):
        cols = pl.ds(chunk * TILE, TILE)
        up, down = self.weights.at[4 + 2 * chunk], self.weights.at[5 + 2 * chunk]
        part = self.rows // 2

        def half(at, carry):
            rows = pl.ds(pl.multiple_of(micro * self.rows + at * part, 16), part)
            hidden = dot_nn(self.normed_two[rows, :], up[...])
            hidden = hidden + self.vector(UB, chunk * TILE, TILE)
            gate = jax.nn.sigmoid(1.702 * hidden)
            self.activated[rows, cols] = (hidden * gate).astype(BF16)
            back = dot_nn(self.proj_back[rows, :], down[...])
            back = back * (gate + 1.702 * hidden * gate * (1.0 - gate))
            back = back.astype(BF16)
            self.pre_back[rows, cols] = back
            self.add_sum(DUB, sum_rows(back.astype(F32)), chunk * TILE)
            return carry

        lax.fori_loop(0, 2, half, 0)

    def out_terms(self, rows, cols):
        return dot_nt(self.mixed[rows, :], self.weights[PO, cols, :])

    def wide_terms(self, ref, first):
        def terms(rows, cols):
            total = None
            for chunk in range(self.chunks):
                one = dot_nt(
                    ref[rows, chunk * TILE : (chunk + 1) * TILE],
                    self.weights[first + 2 * chunk, cols, :],
                )
                total = one if total is None else total + one
            return total

        return terms

    def input_terms(self, rows, cols):
        total = dot_nt(self.queries[rows, :], self.weights[PQ, cols, :])
        total = total + dot_nt(self.keys[rows, :], self.weights[PK, cols, :])
        return total + dot_nt(self.values[rows, :], self.weights[PV, cols, :])

    def enter(self):
        barrier = pltpu.get_barrier_semaphore()
        peers = [self.sib, self.across]
        if self.own_vectors:
            peers.append((self.dp_at, (1 - self.chip_at) * 2 + 1 - self.core_at))
        for peer in peers:
            pl.semaphore_signal(barrier, inc=1, device_id=peer, device_id_type=MESH)
        if self.own_vectors:

            def hail(step):
                peer = (lax.rem(self.dp_at + step, self.dps), self.mp_at)
                pl.semaphore_signal(barrier, inc=1, device_id=peer, device_id_type=MESH)

            each(1, self.dps, hail)
            pl.semaphore_wait(barrier, 3 + self.dps - 1)
        else:
            pl.semaphore_signal(barrier, inc=1, device_id=self.pair, device_id_type=MESH)

            def hail(step):
                peer = self.line_peer(step)
                pl.semaphore_signal(barrier, inc=1, device_id=peer, device_id_type=MESH)

            each(1, self.lines, hail)
            pl.semaphore_wait(barrier, 2 + self.lines)

    def run(self):
        pieces = self.pieces
        last = self.chunks - 1
        self.pack_vectors()
        self.enter()
        if self.own_vectors:
            for step in range(1, self.dps):
                self.vector_copy(step).start()
        for piece in (PQ, PK, PV):
            self.send_weight(piece)
        self.sums[...] = jnp.zeros_like(self.sums)
        self.sums[PEAK : PEAK + 1, :] = jnp.full((1, self.width), -1e30, F32)
        self.take_vectors()
        for micro in (0, 1):
            self.first_norm(micro)
        self.pass_weight(PQ)
        self.pass_weight(PK)
        self.send_weight(PO)
        self.spread_on(0, 0, self.normed_one)
        self.pass_weight(PV)
        self.await_weight(PQ)
        self.spread_on(0, 1, self.normed_one)
        self.project_back(0)
        self.project_back(1)
        self.flush()
        self.send_weight(4)
        self.await_weight(PK)
        self.await_weight(PV)
        self.spread_end(0, 0, self.normed_one)
        self.project_heads(0)
        self.pass_weight(PO)
        self.send_weight(5)
        self.send_weight(6)
        self.spread_end(0, 1, self.normed_one)
        self.project_heads(1)
        self.flush()
        self.attend(0, lambda: None)
        self.await_weight(PO)
        self.collect(0, 0, self.out_terms)
        self.collect_far(0, 0)
        self.pass_weight(4)
        self.send_weight(7)
        self.spread_on(2, 0, self.proj_back)
        self.pass_weight(5)
        self.send_weight(8)
        self.send_pair(9)
        self.attend(1, self.flush)
        self.pass_weight(6)
        self.collect(0, 1, self.out_terms)
        self.collect_far(0, 1)
        self.spread_on(2, 1, self.proj_back)
        self.send_weight(9, False)
        self.second_norm(0)
        self.pass_weight(7)
        self.send_weight(10)
        self.pass_weight(8)
        self.send_weight(11)
        self.second_norm(1)
        self.relay_weight(6)
        self.pass_weight(9)
        self.spread_on(1, 0, self.normed_two)
        self.pass_weight(10)
        self.spread_end(1, 0, self.normed_two)
        self.spread_end(2, 0, self.proj_back)
        self.await_weight(4)
        self.await_weight(5)
        self.feed(0, 0)
        self.await_weight(6)
        self.await_weight(7)
        self.feed(0, 1)
        self.spread_on(1, 1, self.normed_two)
        self.pass_weight(11)
        self.relay_weight(9)

        def up_grad(chunk, send=True):
            cols = slice(chunk * TILE, (chunk + 1) * TILE)
            self.grad_make(4 + 2 * chunk, self.normed_two, self.pre_back[:, cols], send)

        def down_grad(chunk, send=True):
            cols = slice(chunk * TILE, (chunk + 1) * TILE)
            self.grad_make(5 + 2 * chunk, self.proj_back, self.activated[:, cols], send)

        self.await_weight(8)
        self.await_weight(9)
        self.feed(0, 2)
        self.flush()
        self.spread_end(1, 1, self.normed_two)
        self.spread_end(2, 1, self.proj_back)
        self.feed(1, 0)
        self.await_weight(10)
        self.await_weight(11)
        self.feed(0, last)
        self.collect(2, 0, self.wide_terms(self.pre_back, 4))
        self.collect_far(2, 0)
        self.feed(1, 1)
        up_grad(1)
        down_grad(1)
        self.feed(1, 2)
        self.feed(1, last)
        self.collect(2, 1, self.wide_terms(self.pre_back, 4))
        self.second_norm_back(0)
        up_grad(0)
        down_grad(0)
        self.collect_far(2, 1)
        up_grad(2)
        self.collect(1, 0, self.wide_terms(self.activated, 5))
        self.grad_pass(6)
        down_grad(2)
        self.spread_on(3, 0, self.attended_back)
        up_grad(3)
        self.spread_end(3, 0, self.attended_back)

        def between_first():
            self.grad_pass(7)
            self.second_norm_back(1)
            self.grad_relay(4)

        self.attend_back(0, between_first)
        down_grad(3)
        self.grad_pass(8)
        self.collect(3, 0, self.input_terms)
        self.grad_pass(9)
        self.spread_on(3, 1, self.attended_back)
        self.collect_far(3, 0)
        self.spread_sent(2)
        self.grad_relay(5)
        self.spread_end(3, 1, self.attended_back)
        self.grad_make(PO, self.attended_back, self.mixed[...])
        self.grad_pass(10)

        def between_second():
            self.grad_pass(11)
            self.grad_relay(6)
            self.grad_relay(7)

        self.attend_back(1, between_second)
        self.collect(3, 1, self.input_terms)
        self.collect_far(3, 1)
        self.grad_make(PV, self.normed_one, self.values[...])
        self.grad_pass(PO)
        self.grad_cross(4)
        self.grad_cross(5)
        self.grad_make(PQ, self.normed_one, self.queries[...])
        self.grad_make(PK, self.normed_one, self.keys[...])
        self.collect(1, 1, self.wide_terms(self.activated, 5))
        self.collect_far(1, 0)
        self.collect_far(1, 1)
        self.grad_relay(8)
        self.grad_relay(9)
        self.grad_pass(PV)
        self.grad_relay(10)
        self.grad_relay(11)
        self.first_norm_back(0)
        self.first_norm_back(1)
        self.give_vectors()
        self.grad_pass(PQ)
        self.grad_relay(PO)
        self.grad_relay(PV)
        self.grad_pass(PK)
        self.give_result(0)
        for piece in range(4, pieces):
            self.grad_end(piece)
        self.end_vectors()
        self.give_result(1)
        self.last_vectors()
        for piece in (PO, PV, PQ, PK):
            self.grad_end(piece)
        for kind in (0, 1, 3):
            self.spread_sent(kind)
        for one in self.late + self.stage_sends[0] + self.stage_sends[1]:
            one.wait_send()
        for piece in range(pieces):
            self.weight_sent(piece)
            self.grad_sent(piece)
        if self.own_vectors:
            for step in range(1, self.dps):
                self.vector_copy(step).wait_send()
                self.share_copy(step).wait_send()
            for step in range(1, 4):
                self.group_copy(step).wait_send()


def layer_kernel(size, names, *refs):
    named = dict(zip(names, refs))
    named["small"] = [named[name] for name in names if name.startswith("small_")]
    Layer(size, named).run()


def fused_layer(size, counts, tau, images, out_grad, small, weights):
    width, shard, part, rows, pad = (size[key] for key in ("width", "shard", "part", "rows", "pad"))
    lines, dps, pieces = size["lines"], size["dps"], 4 + 2 * size["chunks"]
    units = size["chunks"] * TILE
    vmem = pl.BlockSpec(memory_space=pltpu.VMEM)
    anywhere = pl.BlockSpec(memory_space=pl.ANY)
    vector_shape = (16, 128) if size["own_vectors"] else (16, width)
    outputs = {
        "rows_g": ((2,) + images.shape, BF16),
        "weight_g": ((shard, pieces * TILE + 2 * TILE), F32),
        "vector_g": (vector_shape, F32),
    }
    four = lines == 4
    channels = pieces + (len(PAIR_FIRST) if four else 0)
    pair_slots = pieces * lines - (len(LINE_FIRST) * (lines - 1) if four else 0)
    sum_channels = pieces + (len(LINE_FIRST) if four else 0)
    lines_in = 4 if four else lines - 1
    dma = pltpu.SemaphoreType.DMA
    vm = pltpu.VMEM
    scratch = {
        "weights": vm((pieces, width, TILE), BF16),
        "normed_one": vm((2 * rows, width), BF16),
        "normed_two": vm((2 * rows, width), BF16),
        "proj_back": vm((2 * rows, width), BF16),
        "attended_back": vm((2 * rows, width), BF16),
        "queries": vm((2 * rows, TILE), BF16),
        "keys": vm((2 * rows, TILE), BF16),
        "values": vm((2 * rows, TILE), BF16),
        "mixed": vm((2 * rows, TILE), BF16),
        "mixed_turned": vm((2, TILE, rows), F32),
        "log_total": vm((2, size["heads"], rows), F32),
        "activated": vm((2 * rows, units), BF16),
        "pre_back": vm((2 * rows, units), BF16),
        "turned": vm((TILE, 2 * rows), BF16),
        "mixed_back": vm((rows, TILE), BF16),
        "key_sum": vm((rows, TILE), F32),
        "value_sum": vm((rows, TILE), F32),
        "probs": vm((rows, rows), BF16),
        "score_back": vm((rows, rows), BF16),
        "stage": vm((2, 2, pad, width), BF16),
        "keep": vm((2, 2, 2, pad, width), F32),
        "sib_in": vm((4, 2, 2, pad, width), BF16),
        "far_in": vm((4, 2, pad, width), BF16),
        "after_attn": vm((2, part, width), F32),
        "attn_back": vm((2, part, width), F32),
        "wide_sums": vm((pieces - 4, width, TILE), BF16),
        "pair_in": vm((pair_slots, shard, TILE), BF16),
        "line_in": vm((sum_channels, lines_in, shard, TILE), BF16),
        "vectors": vm((16, width), F32),
        "sums": vm((16, width), F32),
        "wz_send": dma((channels, lines_in)),
        "wz_recv": dma((channels, lines - 1)),
        "wx_send": dma((pieces, lines)),
        "wx_recv": dma((pieces, lines)),
        "wl_sem": dma((pieces,)),
        "ag_send": dma((4, 2, 3)),
        "ag_recv": dma((4, 2, 3)),
        "rs_send": dma((4, 2, 3)),
        "rs_recv": dma((4, 2, 3)),
        "gx_send": dma((pieces, lines)),
        "gx_recv": dma((pieces, lines)),
        "gz_send": dma((sum_channels, lines - 1)),
        "gz_recv": dma((sum_channels, lines_in)),
    }
    if size["own_vectors"]:
        scratch |= {
            "own_packed": vm((16, 128), F32),
            "vectors_in": vm((dps, 16, 128), F32),
            "shares": vm((dps, 16, 128), F32),
            "shares_in": vm((dps - 1, 16, 128), F32),
            "group": vm((4, 16, 128), F32),
            "v_send": dma((2, dps - 1)),
            "v_recv": dma((2, dps - 1)),
            "m_send": dma((3,)),
            "m_recv": dma((3,)),
        }
    inputs = ["counts", "tau", "images", "out_grad"] + [f"small_{at}" for at in range(len(small))]
    inputs += ["query_w", "key_w", "value_w", "out_w", "up_w", "down_w"]
    names = inputs + list(outputs) + list(scratch)
    return pl.pallas_call(
        functools.partial(layer_kernel, size, names),
        out_shape=[jax.ShapeDtypeStruct(*spec) for spec in outputs.values()],
        in_specs=[pl.BlockSpec(memory_space=pltpu.SMEM)] * 2
        + [vmem] * (2 + len(small))
        + [anywhere] * 6,
        out_specs=[vmem] * len(outputs),
        scratch_shapes=list(scratch.values()),
        compiler_params=pltpu.CompilerParams(
            collective_id=0, has_side_effects=True, vmem_limit_bytes=65024 * 2**10
        ),
    )(counts, tau, images, out_grad, *small, *weights)


def on_device(
    images,
    counts,
    first_gain,
    first_shift,
    query_weight,
    query_bias,
    key_weight,
    value_weight,
    value_bias,
    out_weight,
    out_bias,
    second_gain,
    second_shift,
    up_weight,
    up_bias,
    down_weight,
    down_bias,
    clip_tau,
    out_grad,
):
    part, width = images.shape[2:]
    dps = lax.axis_size("dp")
    dp_at = lax.axis_index("dp")
    shard = query_weight.shape[0]
    pad = (part + 15) // 16 * 16
    size = {
        "width": width,
        "shard": shard,
        "part": part,
        "pad": pad,
        "rows": pad * lax.axis_size("mp"),
        "dps": dps,
        "lines": dps // 2,
        "heads": query_weight.shape[1] // HD,
        "chunks": up_weight.shape[1] // TILE,
        "own_vectors": shard == 128,
    }
    bias_cols = query_bias.shape[1]
    parts = [first_gain, first_shift, out_bias, second_gain, second_shift, down_bias, up_bias[0]]
    if size["own_vectors"]:
        small = [one.reshape(1, -1) for one in parts] + [query_bias, value_bias]
    else:
        whole = [lax.all_gather(one, "dp", axis=0, tiled=True) for one in parts]
        rest = [
            jnp.pad(lax.all_gather(one[0], "dp", axis=0, tiled=True), (0, width - TILE))
            for one in (query_bias, value_bias)
        ]
        filler = jnp.zeros((width,), BF16)
        small = [jnp.stack(whole + [filler] + rest + [filler] * 6).astype(F32)]
    weights = (query_weight, key_weight, value_weight, out_weight, up_weight, down_weight)
    rows_g, weight_g, vector_g = fused_layer(
        size, counts.reshape(-1), clip_tau.reshape(1, 1), images, out_grad, small, weights
    )
    columns, units = query_weight.shape[1], up_weight.shape[1]
    edges = [0, columns, 2 * columns, 3 * columns, 4 * columns]
    edges += [edges[-1] + units, edges[-1] + 2 * units]
    query_g, key_g, value_g, out_g, up_g, down_g = (
        weight_g[:, low:high] for low, high in zip(edges[:-1], edges[1:])
    )
    if size["own_vectors"]:
        vectors = [vector_g[row] for row in range(7)]
        query_bias_g = vector_g[DQB : DQB + 1, :bias_cols]
        value_bias_g = vector_g[DVB : DVB + 1, :bias_cols]
        peaks = vector_g[PEAK, : size["heads"]]
        clipped_query = weight_g[:, edges[-1] : edges[-1] + columns]
        clipped_key = weight_g[:, edges[-1] + columns :]
        clipped_bias = vector_g[PEAK + 1 : PEAK + 2, :bias_cols]
    else:
        mine = vector_g[:DUB]
        mine = lax.psum(mine, "mp")
        mine = lax.psum_scatter(mine, "dp", scatter_dimension=1, tiled=True)
        up_bias_g = lax.psum_scatter(vector_g[DUB], "dp", scatter_dimension=0, tiled=True)
        vectors = [mine[row] for row in range(6)] + [up_bias_g]
        both = vector_g[DQB : DVB + 1, :TILE]
        both = lax.psum_scatter(both, "dp", scatter_dimension=1, tiled=True)
        query_bias_g, value_bias_g = both[0:1], both[1:2]
        peaks = lax.pmax(vector_g[PEAK, : size["heads"]], "dp")
        head_root = jnp.sqrt(clip_tau / jnp.maximum(peaks, clip_tau))
        column_root = jnp.repeat(head_root, HD)
        clipped_query = query_weight.astype(F32) * column_root[None, :]
        clipped_key = key_weight.astype(F32) * column_root[None, :]
        bias_root = lax.dynamic_slice(column_root, (dp_at * bias_cols,), (bias_cols,))
        clipped_bias = query_bias.astype(F32) * bias_root[None, :]
    return (
        rows_g[0],
        rows_g[1],
        vectors[DG1],
        vectors[DS1],
        query_g,
        query_bias_g,
        key_g,
        value_g,
        value_bias_g,
        out_g,
        vectors[DOB],
        vectors[DG2],
        vectors[DS2],
        up_g,
        vectors[DUB][None, :],
        down_g,
        vectors[DDB],
        peaks,
        clipped_query,
        clipped_key,
        clipped_bias,
    )


def solution(mesh):
    rows = P(None, "dp", "mp", None)
    wide, small, bias = P("dp", "mp"), P("dp"), P("mp", "dp")
    return jax.shard_map(
        on_device,
        mesh=mesh,
        in_specs=(
            rows,
            P(None, "dp"),
            small,
            small,
            wide,
            bias,
            wide,
            wide,
            bias,
            wide,
            small,
            small,
            small,
            wide,
            bias,
            wide,
            small,
            P(),
            rows,
        ),
        out_specs=(
            rows,
            rows,
            small,
            small,
            wide,
            bias,
            wide,
            wide,
            bias,
            wide,
            small,
            small,
            small,
            wide,
            bias,
            wide,
            small,
            P("mp"),
            wide,
            wide,
            bias,
        ),
        check_vma=False,
    )
```

profile of v0, /device:TPU:0, one launch (start us, length us, event | category | flops | bytes accessed | tf_op | source)
XLA Modules:
  0.0 177.0 jit_solution(2908355110431575565)
XLA Ops:
  1.3 169.6 %shard_map.346 = (bf16[2,2,1,152,1024]{4,3,2,1,0:T(8,128)(2,1)}, f32[128,3584]{1,0:T(8,128)}, f32[16,128]{1,0:T(8,128)}) custom-call(s32[2]{0:T(128)} %bitcast.31, f32[1,1]{1,0:T(1,128)} %bitcast.30.refs_1_, bf16[2,1,152,1024]{3,2,1,0:T(8,128)(2,1)} %refs_2_.1, bf16[2,1,152,1024]{3,2,1,0:T(8,128)(2,1)} %refs_3_.1, bf16[1,128]{1,0:T(2,128)(2,1)} %bitcast.32, ...), custom_call_target="tpu_custom_call" | custom-call | tf_op jit(solution)/shard_map/pallas_call | solution.py:1190
  170.9 0.0 copy-start.1
  170.9 0.0 copy-start
  171.0 2.5 %slice_bitcast_fusion = (bf16[2,1,152,1024]{3,2,1,0:T(8,128)(2,1)}, bf16[2,1,152,1024]{3,2,1,0:T(8,128)(2,1)}) fusion(bf16[2,2,1,152,1024]{4,3,2,1,0:T(8,128)(2,1)} %get-tuple-element.24), kind=kLoop, calls=%fused_computation | loop fusion | bytes 2490368
  173.5 0.0 copy-done.1
  173.5 0.5 slice_bitcast_fusion.2
  174.0 0.5 fusion.2
  174.5 0.5 slice_bitcast_fusion.3
  175.0 0.0 copy-done
  175.1 0.9 fusion
  175.9 1.1 fusion.1
Async XLA Ops:
  170.9 2.5 %copy-start.1 = (f32[16,128]{1,0:T(8,128)S(1)}, f32[16,128]{1,0:T(8,128)}, u32[]{:S(2)}) copy-start(f32[16,128]{1,0:T(8,128)} %get-tuple-element.25) | copy-start | bytes 24580
  170.9 4.1 %copy-start = (f32[128,3584]{1,0:T(8,128)S(1)}, f32[128,3584]{1,0:T(8,128)}, u32[]{:S(2)}) copy-start(f32[128,3584]{1,0:T(8,128)} %get-tuple-element.26) | copy-start | bytes 5505028
where the time goes:
time: 177 us
  Pallas kernels  170 us (96%)
  local copies, waits for them, and re-layouts  6.03 us (3%)
    pallas_call x1, Pallas kernels, fused_layer(): pl.pallas_call(functools.partial(layer_kernel, size, names), out_shape=[j...  170 us

commit v1 on v0

--- a/solution.py
+++ b/solution.py
@@ -16,7 +16,7 @@
 TILE = 256
 PQ, PK, PV, PO = 0, 1, 2, 3
 PAIR_FIRST = (6, 9)
-LINE_FIRST = (4, 5)
+LINE_FIRST = (4, 5, 8)
 DIRECT = (0, 1)
 G1, S1, OB, G2, S2, DB, UB, QB, VB = 0, 1, 2, 3, 4, 5, 6, 8, 9
 DG1, DS1, DOB, DG2, DS2, DDB, DUB, DQB, DVB, PEAK = 0, 1, 2, 3, 4, 5, 6, 7, 8, 9
@@ -1009,6 +1009,8 @@
         self.spread_end(1, 1, self.normed_two)
         self.spread_end(2, 1, self.proj_back)
         self.feed(1, 0)
+        up_grad(0)
+        down_grad(0)
         self.await_weight(10)
         self.await_weight(11)
         self.feed(0, last)
@@ -1021,13 +1023,11 @@
         self.feed(1, last)
         self.collect(2, 1, self.wide_terms(self.pre_back, 4))
         self.second_norm_back(0)
-        up_grad(0)
-        down_grad(0)
+        up_grad(2)
+        down_grad(2)
         self.collect_far(2, 1)
-        up_grad(2)
         self.collect(1, 0, self.wide_terms(self.activated, 5))
         self.grad_pass(6)
-        down_grad(2)
         self.spread_on(3, 0, self.attended_back)
         up_grad(3)
         self.spread_end(3, 0, self.attended_back)
@@ -1039,7 +1039,6 @@
 
         self.attend_back(0, between_first)
         down_grad(3)
-        self.grad_pass(8)
         self.collect(3, 0, self.input_terms)
         self.grad_pass(9)
         self.spread_on(3, 1, self.attended_back)
@@ -1054,6 +1053,7 @@
             self.grad_pass(11)
             self.grad_relay(6)
             self.grad_relay(7)
+            self.grad_relay(8)
 
         self.attend_back(1, between_second)
         self.collect(3, 1, self.input_terms)
@@ -1067,9 +1067,9 @@
         self.collect(1, 1, self.wide_terms(self.activated, 5))
         self.collect_far(1, 0)
         self.collect_far(1, 1)
-        self.grad_relay(8)
         self.grad_relay(9)
         self.grad_pass(PV)
+        self.grad_cross(8)
         self.grad_relay(10)
         self.grad_relay(11)
         self.first_norm_back(0)

time: 177 us -> 175 us (0.989)
  Pallas kernels: 170 us -> 167 us
    pallas_call x1, Pallas kernels: 170 us -> 167 us  [fused_layer(): pl.pallas_call(functools.partial(layer_kernel, size, names), out_shape=[j...]
where the time goes in v1:
time: 175 us
  Pallas kernels  167 us (95%)
  local copies, waits for them, and re-layouts  6.03 us (3%)
    pallas_call x1, Pallas kernels, fused_layer(): pl.pallas_call(functools.partial(layer_kernel, size, names), out_shape=[j...  167 us

profile of v1, /device:TPU:0, one launch (start us, length us, event | category | flops | bytes accessed | tf_op | source)
XLA Modules:
  0.0 174.5 jit_solution(12350080361262742436)
XLA Ops:
  1.3 167.1 %shard_map.346 = (bf16[2,2,1,152,1024]{4,3,2,1,0:T(8,128)(2,1)}, f32[128,3584]{1,0:T(8,128)}, f32[16,128]{1,0:T(8,128)}) custom-call(s32[2]{0:T(128)} %bitcast.31, f32[1,1]{1,0:T(1,128)} %bitcast.30.refs_1_, bf16[2,1,152,1024]{3,2,1,0:T(8,128)(2,1)} %refs_2_.1, bf16[2,1,152,1024]{3,2,1,0:T(8,128)(2,1)} %refs_3_.1, bf16[1,128]{1,0:T(2,128)(2,1)} %bitcast.32, ...), custom_call_target="tpu_custom_call" | custom-call | tf_op jit(solution)/shard_map/pallas_call | solution.py:1190
  168.5 0.0 copy-start.1
  168.5 0.0 copy-start
  168.5 2.5 %slice_bitcast_fusion = (bf16[2,1,152,1024]{3,2,1,0:T(8,128)(2,1)}, bf16[2,1,152,1024]{3,2,1,0:T(8,128)(2,1)}) fusion(bf16[2,2,1,152,1024]{4,3,2,1,0:T(8,128)(2,1)} %get-tuple-element.24), kind=kLoop, calls=%fused_computation | loop fusion | bytes 2490368
  171.0 0.0 copy-done.1
  171.0 0.5 slice_bitcast_fusion.2
  171.5 0.5 fusion.2
  172.0 0.5 slice_bitcast_fusion.3
  172.6 0.0 copy-done
  172.6 0.9 fusion
  173.5 1.1 fusion.1
Async XLA Ops:
  168.5 2.5 %copy-start.1 = (f32[16,128]{1,0:T(8,128)S(1)}, f32[16,128]{1,0:T(8,128)}, u32[]{:S(2)}) copy-start(f32[16,128]{1,0:T(8,128)} %get-tuple-element.25) | copy-start | bytes 24580
  168.5 4.1 %copy-start = (f32[128,3584]{1,0:T(8,128)S(1)}, f32[128,3584]{1,0:T(8,128)}, u32[]{:S(2)}) copy-start(f32[128,3584]{1,0:T(8,128)} %get-tuple-element.26) | copy-start | bytes 5505028

commit v2 on v1

--- a/solution.py
+++ b/solution.py
@@ -228,23 +228,22 @@
             self.broad_each(piece, channel, other, lambda one: one.start())
             return
 
-        def one(step, last=False):
-            self.broad_in(piece, piece, False, step).wait_recv()
-            if last:
-                self.relay(piece, piece, False, lambda one: one.start())
-            self.weight_pair(piece, step, False).start()
-
         if self.lines == 4:
-            second = jnp.where(self.line_at < 2, 3, 1)
-            one(2, True)
-            one(second)
-            self.rest = lambda: one(4 - second)
+            self.pass_shard(piece, 2)
+            self.pass_shard(piece, jnp.where(self.line_at < 2, 3, 1))
+            self.rest = piece
         else:
-            each(1, self.lines, one)
+            each(1, self.lines, lambda step: self.pass_shard(piece, step))
+
+    def pass_shard(self, piece, step):
+        self.broad_in(piece, piece, False, step).wait_recv()
+        if self.lines == 4 and isinstance(step, int):
+            self.relay(piece, piece, False, lambda one: one.start())
+        self.weight_pair(piece, step, False).start()
 
     def flush(self):
         if self.rest is not None:
-            self.rest()
+            self.pass_shard(self.rest, jnp.where(self.line_at < 2, 1, 3))
         self.rest = None
 
     def relay_weight(self, piece):
@@ -963,10 +962,9 @@
         self.pass_weight(4)
         self.send_weight(7)
         self.spread_on(2, 0, self.proj_back)
-        self.pass_weight(5)
         self.send_weight(8)
         self.send_pair(9)
-        self.attend(1, self.flush)
+        self.attend(1, lambda: self.pass_weight(5))
         self.pass_weight(6)
         self.collect(0, 1, self.out_terms)
         self.collect_far(0, 1)

time: 175 us -> 175 us (level)
  no operation moved by 1% of the time
where the time goes in v2:
time: 175 us; the launch traced here: 174 us
  Pallas kernels  167 us (95%)
  local copies, waits for them, and re-layouts  6.03 us (3%)
    pallas_call x1, Pallas kernels, fused_layer(): pl.pallas_call(functools.partial(layer_kernel, size, names), out_shape=[j...  167 us

profile of v2, /device:TPU:0, one launch (start us, length us, event | category | flops | bytes accessed | tf_op | source)
XLA Modules:
  0.0 174.5 jit_solution(1213481619885814615)
XLA Ops:
  1.3 167.1 %shard_map.346 = (bf16[2,2,1,152,1024]{4,3,2,1,0:T(8,128)(2,1)}, f32[128,3584]{1,0:T(8,128)}, f32[16,128]{1,0:T(8,128)}) custom-call(s32[2]{0:T(128)} %bitcast.31, f32[1,1]{1,0:T(1,128)} %bitcast.30.refs_1_, bf16[2,1,152,1024]{3,2,1,0:T(8,128)(2,1)} %refs_2_.1, bf16[2,1,152,1024]{3,2,1,0:T(8,128)(2,1)} %refs_3_.1, bf16[1,128]{1,0:T(2,128)(2,1)} %bitcast.32, ...), custom_call_target="tpu_custom_call" | custom-call | tf_op jit(solution)/shard_map/pallas_call | solution.py:1188
  168.4 0.0 copy-start.1
  168.4 0.0 copy-start
  168.5 2.5 %slice_bitcast_fusion = (bf16[2,1,152,1024]{3,2,1,0:T(8,128)(2,1)}, bf16[2,1,152,1024]{3,2,1,0:T(8,128)(2,1)}) fusion(bf16[2,2,1,152,1024]{4,3,2,1,0:T(8,128)(2,1)} %get-tuple-element.24), kind=kLoop, calls=%fused_computation | loop fusion | bytes 2490368
  171.0 0.0 copy-done.1
  171.0 0.5 slice_bitcast_fusion.2
  171.5 0.5 fusion.2
  172.0 0.5 slice_bitcast_fusion.3
  172.5 0.0 copy-done
  172.6 0.9 fusion
  173.4 1.1 fusion.1
Async XLA Ops:
  168.4 2.5 %copy-start.1 = (f32[16,128]{1,0:T(8,128)S(1)}, f32[16,128]{1,0:T(8,128)}, u32[]{:S(2)}) copy-start(f32[16,128]{1,0:T(8,128)} %get-tuple-element.25) | copy-start | bytes 24580
  168.4 4.1 %copy-start = (f32[128,3584]{1,0:T(8,128)S(1)}, f32[128,3584]{1,0:T(8,128)}, u32[]{:S(2)}) copy-start(f32[128,3584]{1,0:T(8,128)} %get-tuple-element.26) | copy-start | bytes 5505028
